TPU v7x, 256 devices: a whole 4x4x8 slice. The times are simulated.
256 devices in a mesh: val: 4 (over z_hi), cond: 64 (over y, z_lo, x, core).
Axes of the slice: x: 4, y: 4, z: 8 (z_hi: 4, z_lo: 2; z = z_hi * 2 + z_lo), core: 2. Of those that a mesh axis runs over, the one named last changes fastest.
Arguments:
- val_orbitals: bfloat16 [4, 262144], P('val', 'cond'), may hold values from -6 to 6
- cond_orbitals: bfloat16 [64, 262144], P('cond', 'val'), may hold values from -6 to 6
- val_energy: float32 [4], P('val'), may hold values from -3 to -0.2
- cond_energy: float32 [64], P('cond'), may hold values from 0.5 to 5
- plane_index: int32 [19968], replicated, may hold values from 0 to 262143, as said below
- column_index: int32 [2048], replicated, may hold values from 0 to 19967, as said below
Outputs:
- chi_block: float32 [19968, 2048], P('cond', 'val')
Inputs may be any that keep to these rules, and one draw needn't show every extreme that they name: `plane_index`: distinct grid indices; 0 and 262143 are always among them. `column_index`: distinct plane-wave indices; 0 and 19967 are always among them.
All inputs are finite; a program needn't handle non-finite values.
Results may differ from a plain program's by a relative error of at most 0.014.
Values may be sent and summed in bfloat16 or wider, within the bound.
A program may use at most 64 MiB of HBM per device.

v0:
```python
import math

import jax
import jax.numpy as jnp
from jax import lax
from jax.sharding import PartitionSpec as P

NFFT = 64


def dft_tables(length):
    steps = jnp.arange(length, dtype=jnp.int32)
    phase = steps[:, None] * steps[None, :] % length
    angle = phase.astype(jnp.float32) * (2.0 * math.pi / length)
    return (jnp.cos(angle), jnp.sin(angle))


def transform(density):
    cosine, sine = dft_tables(NFFT)
    level = lax.Precision.HIGH
    real_part = jnp.einsum("pxyz,zk->pxyk", density, cosine, precision=level)
    imag_part = -jnp.einsum("pxyz,zk->pxyk", density, sine, precision=level)
    for form in ("pxyk,yw->pxwk", "pxyk,xw->pwyk"):
        new_real = jnp.einsum(form, real_part, cosine, precision=level) + jnp.einsum(
            form, imag_part, sine, precision=level
        )
        new_imag = jnp.einsum(form, imag_part, cosine, precision=level) - jnp.einsum(
            form, real_part, sine, precision=level
        )
        real_part, imag_part = (new_real, new_imag)
    pairs = density.shape[0]
    return (real_part.reshape(pairs, -1), imag_part.reshape(pairs, -1))


def contract(rows, columns):
    return -lax.dot_general(
        rows, columns, (((0,), (0,)), ((), ())), preferred_element_type=jnp.float32
    )


def on_device(val_orbitals, cond_orbitals, val_energy, cond_energy, plane_index, column_index):
    whole_val = lax.all_gather(val_orbitals, "cond", axis=1, tiled=True)
    whole_cond = lax.all_gather(cond_orbitals, "val", axis=1, tiled=True)
    val_count = whole_val.shape[0]
    cond_count = whole_cond.shape[0]
    density = whole_val.astype(jnp.float32)[:, None, :] * whole_cond.astype(jnp.float32)[None, :, :]
    density = density.reshape(val_count * cond_count, NFFT, NFFT, NFFT)
    real_part, imag_part = transform(density)
    picked_real = jnp.take(real_part, plane_index, axis=1)
    picked_imag = jnp.take(imag_part, plane_index, axis=1)
    total_pairs = val_count * lax.axis_size("val") * cond_count * lax.axis_size("cond")
    weight = 1.0 / (cond_energy[None, :] - val_energy[:, None])
    factor = jnp.sqrt(weight / (math.sqrt(total_pairs) * NFFT**3)).reshape(-1)
    values = jnp.concatenate(
        [picked_real * factor[:, None], picked_imag * factor[:, None]], 0
    ).astype(jnp.bfloat16)
    row_values = lax.all_to_all(values, "cond", split_axis=1, concat_axis=0, tiled=True)
    col_values = lax.all_gather(jnp.take(values, column_index, axis=1), "cond", axis=0, tiled=True)
    partial_block = contract(row_values, col_values)
    return lax.psum_scatter(
        partial_block.astype(jnp.bfloat16), "val", scatter_dimension=1, tiled=True
    ).astype(jnp.float32)


def solution(mesh):
    placed = (P("val", "cond"), P("cond", "val"), P("val"), P("cond"), P(), P())
    return jax.shard_map(
        on_device, mesh=mesh, in_specs=placed, out_specs=P("cond", "val"), check_vma=False
    )
```

profile of v0, /device:TPU:33, one launch (start us, length us, event | category | flops | bytes accessed | tf_op | source)
XLA Modules:
  0.0 502.7 jit_solution(11993492139345946370)
XLA Ops:
  6.5 24.9 %all_gather.10 = bf16[1,262144]{1,0:T(2,128)(2,1)S(1)} all-gather(bf16[1,65536]{1,0:T(2,128)(2,1)} %param.9), channel_id=1, replica_groups=mesh['val'=4,'cond'=64] {'val'}, dimensions={1}, use_global_device_ids=true | all-gather | bytes 655360 | tf_op jit(solution)/shard_map/all_gather | solution.py:43
  31.4 79.7 %all_gather.9 = bf16[1,262144]{1,0:T(2,128)(2,1)S(1)} all-gather(bf16[1,4096]{1,0:T(2,128)(2,1)} %param.8), channel_id=1, replica_groups=mesh['val'=4,'cond'=64] {'cond'}, dimensions={1}, use_global_device_ids=true | all-gather | bytes 532480 | tf_op jit(solution)/shard_map/all_gather | solution.py:42
  111.1 10.9 %multiply_reduce_fusion = f32[262144]{0:T(1024)S(1)} fusion(bf16[1,262144]{1,0:T(2,128)(2,1)S(1)} %all_gather.10, bf16[1,262144]{1,0:T(2,128)(2,1)S(1)} %all_gather.9), kind=kLoop, calls=%fused_computation.21 | loop fusion | flops 786432 | bytes 2097152 | tf_op jit(solution)/shard_map/mul | solution.py:46
  122.0 0.3 mul.124
  122.3 1.1 fusion.35
  123.5 1.1 fusion.28
  124.6 1.1 fusion.40
  125.7 1.1 fusion.32
  126.8 1.2 subtract_bitcast_fusion
  128.0 2.2 fusion.3
  130.2 3.6 fusion.1
  133.8 1.2 add_bitcast_fusion
  135.0 2.5 fusion.17
  137.5 2.5 copy.29
  140.0 1.8 reshape.131
  141.9 102.6 %gather_fusion.1 = f32[19968]{0:T(1024)S(1)} fusion(f32[262144]{0:T(1024)S(1)} %reshape.131, s32[20480]{0:T(1024)S(1)} %pad_clamp_fusion), kind=kCustom, calls=%fused_computation.clone | custom fusion | bytes 239616 | tf_op jit(solution)/shard_map/jit(_take)/gather | solution.py:49
  244.5 3.9 fusion.20
  248.4 1.2 copy.32
  249.6 0.3 reshape.134
  249.9 102.6 %gather_fusion.2 = f32[19968]{0:T(1024)S(1)} fusion(f32[262144]{0:T(1024)S(1)} %reshape.134, s32[20480]{0:T(1024)S(1)} %pad_clamp_fusion), kind=kCustom, calls=%fused_computation.1.clone | custom fusion | bytes 239616 | tf_op jit(solution)/shard_map/jit(_take)/gather | solution.py:50
  353.9 0.5 fusion.98
  354.7 0.7 copy.33
  355.5 12.3 %all-to-all-start = ((bf16[2,64,312]{2,0,1:T(2,128)(2,1)}), bf16[2,64,312]{2,0,1:T(2,128)(2,1)S(1)}, u32[]{:S(2)}, u32[]{:S(2)}) async-start(bf16[2,64,312]{2,0,1:T(2,128)(2,1)} %copy.33), calls=%async_computation | async-start | bytes 196608 | tf_op jit(solution)/shard_map/all_to_all | solution.py:57
  368.0 3.7 copy.34
  371.7 8.7 %gather_fusion = bf16[2048,2]{1,0:T(8,128)(2,1)S(1)} fusion(bf16[2,19968]{0,1:T(8,128)(2,1)} %copy.34, s32[2048]{0:T(1024)S(1)} %fusion.57), kind=kCustom, calls=%fused_computation.2 | custom fusion | bytes 24576 | tf_op jit(solution)/shard_map/jit(_take)/gather | solution.py:58
  380.4 0.3 select_bitcast_fusion
  380.8 0.2 copy.35
  381.0 75.9 %all-gather = bf16[64,2,2048]{2,1,0:T(2,128)(2,1)S(1)} all-gather(bf16[1,2,2048]{2,1,0:T(2,128)(2,1)S(1)} %copy.35), channel_id=1, replica_groups=mesh['val'=4,'cond'=64] {'cond'}, dimensions={0}, use_global_device_ids=true | all-gather | bytes 532480 | tf_op jit(solution)/shard_map/all_gather | solution.py:58
  456.9 0.2 reshape.130
  457.2 1.6 fusion
  458.8 35.2 %reduce-scatter.2.cloned.1.call-done = bf16[312,512]{1,0:T(8,128)(2,1)} async-done(((bf16[312,2048]{1,0:T(8,128)(2,1)}), bf16[312,512]{1,0:T(8,128)(2,1)}) %reduce-scatter.2.cloned.1.call-update) | async-done | bytes 319504 | tf_op jit(solution)/shard_map/reduce_scatter | solution.py:60
  493.9 1.9 convert_element_type.39
  (18 shorter events, 0.7 us)
Async XLA Ops:
  140.0 1.8 copy-start
  249.9 117.9 %copy-start.1 = (s32[2048]{0:T(1024)S(1)}, s32[2048]{0:T(1024)}, u32[]{:S(2)}) copy-start(s32[2048]{0:T(1024)} %param.13) | copy-start | bytes 24580
  355.5 101.6 %all-to-all-start = ((bf16[2,64,312]{2,0,1:T(2,128)(2,1)}), bf16[2,64,312]{2,0,1:T(2,128)(2,1)S(1)}, u32[]{:S(2)}, u32[]{:S(2)}) async-start(bf16[2,64,312]{2,0,1:T(2,128)(2,1)} %copy.33), calls=%async_computation | async-start | bytes 196608 | tf_op jit(solution)/shard_map/all_to_all | solution.py:57
  367.8 126.2 %reduce-scatter.2.cloned.1.call-start = ((), (), s32[]{:S(2)}) async-start(), calls=%async_computation.2 | async-start | bytes 1597440 | tf_op jit(solution)/shard_map/reduce_scatter | solution.py:60
Sparse Core Ops, SparseCore 0:
  458.9 34.9 reduce-scatter.1
where the time goes:
time: 507 us; the launch traced here: 503 us
  local copies, waits for them, and re-layouts  225 us (44%)
  blocking collectives  180 us (36%)
  waiting for transfers between devices  35.2 us (7%)
  matrix products  20.5 us (4%)
  between operations  15 us (3%)
  other arithmetic  13.9 us (3%)
  starting transfers between devices  12.3 us (2%)
    gather x1, local copies, waits for them, and re-layouts, on_device(): picked_real = jnp.take(real_part, plane_index, axis=1)  103 us
    gather x1, local copies, waits for them, and re-layouts, on_device(): picked_imag = jnp.take(imag_part, plane_index, axis=1)  103 us
    all_gather x1, blocking collectives, on_device(): whole_val = lax.all_gather(val_orbitals, 'cond', axis=1, tiled=True)  79.7 us
    all_gather x1, blocking collectives, on_device(): lax.all_gather(jnp.take(values, column_index, axis=1), 'cond', axis=0, ti...  75.9 us
    reduce_scatter x1, waiting for transfers between devices, on_device(): lax.psum_scatter(partial_block.astype(jnp.bfloat16), 'val', scatter_dimen...  35.2 us
    all_gather x1, blocking collectives, on_device(): whole_cond = lax.all_gather(cond_orbitals, 'val', axis=1, tiled=True)  24.9 us
    all_to_all x1, starting transfers between devices, on_device(): lax.all_to_all(values, 'cond', split_axis=1, concat_axis=0, tiled=True)  12.3 us
    mul x1, other arithmetic, on_device(): whole_val.astype(jnp.float32)[:, None, :]  10.9 us
  transfers between devices with their start and end apart: 2, of which 1 were waited for; matrix products, arithmetic and copies ran while one was open for 3% of the time, Pallas kernels for 0%

commit v1 on v0

v1 whole, which is shorter than its diff:
```python
import math

import jax
import jax.numpy as jnp
import ml_dtypes
import numpy as np
from jax import lax
from jax.experimental import pallas as pl
from jax.experimental.pallas import tpu as pltpu
from jax.sharding import PartitionSpec as P

N = 64
GRID = N**3
BF = jnp.bfloat16
F32 = jnp.float32
ROWS = 312


def split(a):
    hi = a.astype(ml_dtypes.bfloat16)
    return hi, (a - hi.astype(np.float64)).astype(ml_dtypes.bfloat16)


def tables():
    k = np.arange(N)
    ang = 2 * np.pi * (k[:, None] * k[None, :] % N) / N
    cos, sin = np.cos(ang), np.sin(ang)
    tz = np.zeros((2, N, 2, 2, N))
    for par in range(2):
        tz[par, :, 0, par, :] = cos
        tz[par, :, 1, par, :] = -sin
    tz = tz.reshape(128, 256)
    tz = np.concatenate([tz, tz], 0).astype(ml_dtypes.bfloat16)
    h = np.arange(32)
    ang = 2 * np.pi * (h[:, None] * h[None, :] % 32) / 32
    ty = np.block([[np.cos(ang), np.sin(ang)], [-np.sin(ang), np.cos(ang)]])
    hi, lo = split(ty)
    ty = np.concatenate([hi, lo, hi], 1)
    tx = np.zeros((80, 128))
    tx[:32, :64], tx[:32, 64:] = cos[:32], sin[:32]
    tx[32:64, :64], tx[32:64, 64:] = -sin[:32], cos[:32]
    tx[64, :64] = cos[32]
    tx[65, 64:] = cos[32]
    tx = np.concatenate([tx, tx], 1).astype(ml_dtypes.bfloat16)
    tw = np.zeros((2, 32, 128), np.float32)
    tw[0, :, :64] = 1.0
    ang = 2 * np.pi * h / N
    tw[0, :, 64:] = np.cos(ang)[:, None]
    tw[1, :, 64:] = -np.sin(ang)[:, None]
    return tz, ty, tx, tw


def cond_id(s, xy):
    return (xy // 4) * 16 + (s // 2) * 8 + (xy % 4) * 2 + s % 2


def lanes(shape):
    return lax.broadcasted_iota(jnp.int32, shape, len(shape) - 1)


def subl(shape):
    return lax.broadcasted_iota(jnp.int32, shape, len(shape) - 2)


def order_planes(plane_ref, ix_ref):
    lane = lanes((3, 128))

    def take(start):
        row, off = start // 128, start % 128
        a = plane_ref[row : row + 3, :]
        if off:
            if row + 4 <= 156:
                b = plane_ref[row + 1 : row + 4, :]
            else:
                b = jnp.concatenate([plane_ref[row + 1 : row + 3, :], a[2:3]], 0)
            a = jnp.where(lane < 128 - off, pltpu.roll(a, 128 - off, 1), pltpu.roll(b, 128 - off, 1))
        return a

    for s in range(4):
        for m in range(8):
            even = take(ROWS * cond_id(s, 2 * m))
            odd = take(ROWS * cond_id(s, 2 * m + 1) - 64)
            at = 16 + s * 40 + m * 5
            ix_ref[at : at + 2, :] = even[:2]
            ix_ref[at + 2 : at + 3, :] = jnp.where(lane[:1] < 64, even[2:], odd[:1])
            ix_ref[at + 3 : at + 5, :] = odd[1:]


def compose_columns(plane_ref, col_ref, ix_ref):
    plane = jnp.concatenate([plane_ref[...], jnp.zeros((100, 128), jnp.int32)], 0)
    digits = [
        jnp.transpose(((plane >> sh) & 63).astype(F32), (1, 0)).astype(BF) for sh in (12, 6, 0)
    ]
    left = jnp.concatenate(digits, 0)

    def tile(t, carry):
        col = jnp.concatenate([col_ref[pl.ds(2 * t, 1), :], col_ref[pl.ds(2 * t + 1, 1), :]], 1)
        hot = jnp.where(subl((256, 256)) == (col >> 7), 1.0, 0.0).astype(BF)
        prod = jnp.dot(left, hot, preferred_element_type=F32)
        mask = subl((128, 256)) == (col & 127)
        kx, ky, kz = [
            jnp.sum(jnp.where(mask, prod[128 * d : 128 * d + 128], 0.0), axis=0, keepdims=True)
            for d in range(3)
        ]
        flat = (kx * 4096.0 + ky * 64.0 + kz).astype(jnp.int32)
        ix_ref[pl.ds(2 * t, 1), :] = flat[:, :128]
        ix_ref[pl.ds(2 * t + 1, 1), :] = flat[:, 128:]
        return carry

    lax.fori_loop(0, 8, tile, 0, unroll=4)


def fold_indices(ix_ref, fx_ref):
    n = ix_ref[...]
    kx, ky, kz = n >> 12, (n >> 6) & 63, n & 63
    low = (kx & 31) == 0
    yline = (ky & 31) == 0
    zpoint = (kz & 31) == 0
    neg = kx > 32
    neg = neg | (low & ~yline & ((kx == 0) == (ky > 32)))
    neg = neg | (low & yline & ~zpoint & ((ky == 0) == (kz > 32)))
    special = low & yline & zpoint & ((ky == 0) == (kz == 32))
    turn = lambda k: jnp.where(neg, (64 - k) & 63, k)
    kx, ky, kz = turn(kx), turn(ky), turn(kz)
    slot_y = jnp.where(low & yline, kx, ky)
    fx_ref[0] = (kx & 31).astype(F32)
    fx_ref[1] = jnp.where(special, 99, slot_y & 15).astype(F32)
    line = ((slot_y >> 4) & 1) * 128 + (slot_y >> 5) * 64 + kz
    fx_ref[2] = (line & 15).astype(F32)
    fx_ref[5] = (line >> 4).astype(F32)
    fx_ref[3] = jnp.where(neg, -1.0, 1.0)
    fx_ref[4] = jnp.where(special, (kx >> 5) * 2 + (ky >> 5), 9).astype(F32)


def transform(ready, vf, cf, tz, ty, tw, bs):
    low = lanes((32, 128)) < 64

    def planes(n, carry):
        for y, zl in ready(n):
            a = vf[y, zl].reshape(256, 128).astype(F32)
            b = cf[y, pl.ds(pl.multiple_of(zl * 256, 256), 256), :].astype(F32)
            d = a * b
            hi = d.astype(BF)
            lo = (d - hi.astype(F32)).astype(BF)
            az = jnp.dot(jnp.concatenate([hi, lo], 1), tz[...], preferred_element_type=F32)
            for m in range(4):
                cols = []
                for x in (2 * m, 2 * m + 1):
                    blk = az[x * 32 : x * 32 + 32]
                    cols.append(jnp.concatenate([blk[:, :128], blk[:, 128:]], 0))
                r = jnp.concatenate(cols, 1)
                hi = r.astype(BF)
                lo = (r - hi.astype(F32)).astype(BF)
                g = jnp.dot(ty[...], jnp.concatenate([hi, hi, lo], 0), preferred_element_type=F32)
                for e in range(2):
                    gr, gi = g[:32, e * 128 : e * 128 + 128], g[32:, e * 128 : e * 128 + 128]
                    yr = gr * tw[0] - gi * tw[1]
                    yi = gr * tw[1] + gi * tw[0]
                    at = (y * 16 + zl * 8 + 2 * m + e) * 32
                    for part, v in ((0, yr), (1, yi)):
                        rv = pltpu.roll(v, 64, 1)
                        out = jnp.where(low, rv + v, rv - v)
                        bs[pl.ds(pl.multiple_of(part * 2048 + at, 32), 32), :] = out
        return carry

    lax.fori_loop(0, 4, planes, 0)


def lines_of(fac_ref, tx, bs, wt, sp):
    fac = fac_ref[0:1, :]

    def lines(i, carry):
        b = [bs[pl.ds(4 * i + j, 128, stride=32), :] for j in range(4)]
        r = jnp.concatenate(b, 1)
        hi = r.astype(BF)
        lo = (r - hi.astype(F32)).astype(BF)
        f = jnp.dot(tx[...], jnp.concatenate([hi, lo], 0), preferred_element_type=F32)
        lane = lanes((1, 128))
        top = subl((32, 128)) == 0
        for part in range(2):
            blocks = []
            for j in range(4):
                main = f[32 * part : 32 * part + 32, 128 * j : 128 * j + 128] * fac
                edge = f[64 + part : 65 + part, 128 * j : 128 * j + 128] * fac
                row = main[0:1]
                new = jnp.where(lane < 64, row, edge)
                if j == 0:
                    first = jnp.where(
                        lane < 32,
                        row,
                        jnp.where(
                            lane < 64,
                            pltpu.roll(row, 64, 1),
                            jnp.where(lane < 96, pltpu.roll(edge, 64, 1), edge),
                        ),
                    )
                    if part == 0:

                        @pl.when(i == 0)
                        def _():
                            for n, (v, at) in enumerate(
                                ((row, 32), (row, 64), (edge, 32), (edge, 64))
                            ):
                                pick = jnp.sum(
                                    jnp.where(lane == at, v, 0.0), axis=1, keepdims=True
                                )
                                pick = pick.astype(BF).astype(F32)
                                sp[n : n + 1, :] = jnp.broadcast_to(pick, (1, 256))

                    new = jnp.where(i == 0, first, new)
                blocks.append(jnp.where(top, jnp.broadcast_to(new, (32, 128)), main))
            whole = jnp.transpose(jnp.concatenate(blocks, 0), (1, 0)).astype(BF)
            rows = pl.ds(pl.multiple_of(256 * part + (i // 4) * 128, 128), 128)
            wt[rows, pl.ds(pl.multiple_of((i % 4) * 128, 128), 128)] = whole
        return carry

    lax.fori_loop(0, 8, lines, 0, unroll=2)


def pick_tile(t, fx, wt, sp):
    def row(n):
        return jnp.concatenate([fx[n, pl.ds(2 * t, 1), :], fx[n, pl.ds(2 * t + 1, 1), :]], 1)

    kx = jnp.broadcast_to(row(0), (32, 256)).astype(BF)
    ky = jnp.broadcast_to(row(1), (16, 256)).astype(BF)
    index = subl((32, 256)).astype(F32).astype(BF)
    one, zero = jnp.ones((32, 256), BF), jnp.zeros((16, 256), BF)
    base = jnp.where(kx == index, one, jnp.zeros((32, 256), BF))
    hot = []
    for j in range(16):
        here = ky == jnp.asarray(j, BF)
        hot += [jnp.where(here, base[:16], zero), jnp.where(here, base[16:], zero)]
    hot = jnp.concatenate(hot, 0)
    prod = jnp.dot(wt[...], hot, preferred_element_type=F32).astype(BF)
    high = jnp.broadcast_to(row(5), (16, 256)).astype(BF)
    chosen = [prod[:16], prod[256:272]]
    for n in range(1, 16):
        here = high == jnp.asarray(n, BF)
        for part in range(2):
            at = 256 * part + 16 * n
            chosen[part] = jnp.where(here, prod[at : at + 16], chosen[part])
    line = subl((16, 256)).astype(F32) == row(2)
    re, im = [
        jnp.sum(jnp.where(line, v.astype(F32), 0.0), axis=0, keepdims=True) for v in chosen
    ]
    kind = row(4)
    for n in range(4):
        re = jnp.where(kind == float(n), sp[n : n + 1, :], re)
    return re, im * row(3)


def kernel(
    val_in, cond_ref, ve_ref, ce_ref, plane_ref, col_ref, tz, ty, tx, tw,
    rx, cx,
    val_ref, wide, vf, cf, facs, fac, ix, fx, bs, wt, sp, pv, cb, zs, rz, rf, xs,
    s_val, r_val, s_cond, r_cond, s_pass, s_sib, r_sib, s_fac, r_fac,
    s_vf, r_va, r_vb, r_vy, r_vx,
    s_cb, r_cb, s_cx, r_cx, s_cs, r_cs, s_rz, r_rz, r_rw, s_rx, r_rx,
):
    p = lax.axis_index("val")
    c = lax.axis_index("cond")
    y, zl, x, core = c // 16, (c // 8) % 2, (c // 2) % 4, c % 2
    s = zl * 2 + core
    xy = y * 4 + x
    me = s * 4 + p
    base = y * 16 + x * 2
    at_s = lambda n: base + (n >> 1) * 8 + (n & 1)
    by_s = lambda k: c ^ (((k >> 1) << 3) | (k & 1))
    by_xy = lambda k: c ^ (((k >> 2) << 4) | ((k & 3) << 1))
    twin = p == s
    cond_of = lambda o: (c & 9) | ((o >> 2) << 4) | ((o & 3) << 1)

    def remote(src, dst, send, recv, dp, dc):
        return pltpu.make_async_remote_copy(
            src_ref=src, dst_ref=dst, send_sem=send, recv_sem=recv,
            device_id=(dp, dc), device_id_type=pl.DeviceIdType.MESH,
        )

    def put(here, src, dst, send, recv, dp, dc):
        @pl.when(jnp.logical_not(here))
        def _():
            remote(src, dst, send, recv, dp, dc).start()

        @pl.when(here)
        def _():
            pltpu.make_async_copy(src, dst, recv).start()

    def drain(ref, sem):
        pltpu.make_async_copy(ref, ref, sem).wait()

    def drain_bytes(n, sem):
        drain(bs.at[pl.ds(0, n // 512)], sem)

    barrier = pltpu.get_barrier_semaphore()
    for k in range(1, 16):
        for dev in ((p ^ (k >> 2), by_s(k & 3)), (p, by_xy(k))):
            pl.semaphore_signal(
                barrier, inc=1, device_id=dev, device_id_type=pl.DeviceIdType.MESH
            )
    gap = jnp.full((8, 128), ce_ref[0], F32) - jnp.full((8, 128), ve_ref[0], F32)
    facs[...] = jnp.sqrt((1.0 / gap) * (1.0 / (math.sqrt(256.0) * GRID)))
    for i in range(32):
        wide[i : i + 1, :] = val_in[0:1, 128 * i : 128 * i + 128].astype(F32)
    val_ref[...] = wide[...].astype(BF)
    pl.semaphore_wait(barrier, 30)

    half = lambda h: pl.ds(pl.multiple_of(h * 256, 256), 256)
    mine = vf.at[y, zl, x, core]
    put(twin, val_ref, mine, s_val.at[0], r_val, p, at_s(p))
    for k in range(1, 4):
        remote(val_ref, mine, s_val.at[1], r_val, p ^ k, at_s(p)).start()
    put(twin, facs, fac, s_fac, r_fac, s, at_s(p))
    gone = (s - p) & 3
    near = jnp.where(zl == 0, gone >> 1, 1 - (((gone + 1) >> 1) & 1))
    for h in range(2):
        put(
            twin & (core == h), cond_ref.at[half(h)], cf.at[p, half(h)],
            s_cond.at[h], r_cond.at[p], s, at_s(near * 2 + h),
        )

    drain(vf.at[y, :, x], r_val)
    for k in range(1, 4):
        remote(vf.at[y, 0, x], vf.at[y, 0, x], s_vf, r_va, p, by_xy(k)).start()
        remote(vf.at[y, 1, x], vf.at[y, 1, x], s_vf, r_vb, p, by_xy(4 * k)).start()
    drain_bytes(3 * 16384, r_va)
    for k in range(1, 4):
        remote(vf.at[y, 0], vf.at[y, 0], s_vf, r_vy.at[y], p, by_xy(4 * k)).start()
    drain_bytes(3 * 16384, r_vb)
    for k in range(1, 4):
        remote(vf.at[:, 1, x], vf.at[:, 1, x], s_vf, r_vx, p, by_xy(k)).start()

    e1 = jnp.where(p < 2, 2 * zl, 1 + 2 * zl)

    def pass_on(k):
        q = (p - e1 - k) & 3
        part = cf.at[q, half(core)]
        drain(part, r_cond.at[q])
        if k < 2:
            remote(part, part, s_pass, r_cond.at[q], p, c ^ 8).start()
        remote(part, part, s_sib, r_sib.at[q], p, by_s(1)).start()

    pass_on(0)
    pass_on(1)
    order_planes(plane_ref, ix)
    compose_columns(plane_ref, col_ref, ix)
    fold_indices(ix, fx)
    pass_on(2)
    pass_on(3)

    def ready(n):
        o0 = y ^ (2 * (n & 1))
        o1 = o0 ^ 1
        h = core ^ (n >> 1)
        later = (n & 1) == 1

        @pl.when((h == 0) & later)
        def _():
            drain(vf.at[o0, 0], r_vy.at[o0])

        @pl.when(h == 0)
        def _():
            drain(vf.at[o1, 0], r_vy.at[o1])

        @pl.when((h == 1) & jnp.logical_not(later))
        def _():
            drain_bytes(3 * 65536, r_vx)

        @pl.when(n >= 2)
        def _():
            drain(cf.at[o0, half(1 - core)], r_sib.at[o0])
            drain(cf.at[o1, half(1 - core)], r_sib.at[o1])

        return (o0, h), (o1, h)

    transform(ready, vf, cf, tz, ty, tw, bs)
    drain(fac, r_fac)
    lines_of(fac, tx, bs, wt, sp)

    def keep(t, at, step):
        re, im = pick_tile(t, fx, wt, sp)
        pv[pl.ds(at, 1), :] = re[:, :128]
        pv[pl.ds(at + 1, 1), :] = re[:, 128:]
        pv[pl.ds(at + step, 1), :] = im[:, :128]
        pv[pl.ds(at + step + 1, 1), :] = im[:, 128:]

    for t in range(8):
        keep(t, (t // 2) * 8 + (t % 2) * 2, 4)

    slot = lambda n, size: pl.ds(pl.multiple_of(n * size, size), size)
    mine_cb = cb.at[slot(core * 4 + p, 8)]
    for k in range(8):
        to = base + (zl ^ (k & 1)) * 8 + zl
        src = pv.at[slot(p ^ (k >> 1), 8)]
        if k == 0:
            put(core == zl, src, mine_cb, s_cb.at[0], r_cb, p, to)
        else:
            remote(src, mine_cb, s_cb.at[1], r_cb, p ^ (k >> 1), to).start()

    def columns():
        drain(cb, r_cb)
        own = [(-cb[pl.ds(n, 16, stride=4), :]).astype(BF) for n in range(4)]
        cx[pl.ds(xy, 1), pl.ds(core, 1)] = jnp.concatenate(own, 1)[None, None]
        for k in range(1, 16):
            remote(cx.at[xy, core], cx.at[xy, core], s_cx, r_cx, p, by_xy(k)).start()

    def swap_columns():
        drain_bytes(15 * 16384, r_cx)
        remote(cx.at[:, core], cx.at[:, core], s_cs, r_cs, p, by_s(1)).start()

    def send_rows(h, whole):
        for j in range(16):
            if whole:
                v = rz[j, 0:80].astype(F32)[40 * h : 40 * h + 40]
            else:
                v = rz[j, 48 * h : 48 * h + 48].astype(F32)[:40]
            rf[40 * j : 40 * j + 40, :] = v
        low = lanes((32, 128)) < 64
        for m in range(4):
            a = [rf[pl.ds(5 * m + n, 32, stride=20), :] for n in range(5)]
            b = [pltpu.roll(v, 64, 1) for v in a[2:]]
            odd = [jnp.where(low, b[0], b[1]), jnp.where(low, b[1], b[2]), b[2]]
            xs[8 * h + 2 * m] = jnp.concatenate(a[:3], 1).astype(BF)
            xs[8 * h + 2 * m + 1] = jnp.concatenate(odd, 1).astype(BF)
        for k in range(8):
            o = 8 * h + (k ^ (xy & 7))

            @pl.when(o != xy)
            def _():
                remote(xs.at[o], rx.at[xy], s_rx, r_rx, p, cond_of(o)).start()

            @pl.when(o == xy)
            def _():
                rx[pl.ds(xy, 1)] = xs[pl.ds(xy, 1)]

    def rows_to(g, src, dst, recv):
        put(g == s, src, dst, s_rz, recv, p, at_s(g))
        for j in range(1, 4):
            remote(src, dst, s_rz, recv, p ^ j, at_s(g)).start()

    swap = lambda n: ((n & 1) << 1) | (n >> 1)

    def pick(b, carry):
        k, w = b // 2, b % 2
        g = swap(k)
        for e in range(10):
            keep(8 + g * 20 + w * 10 + e, 32 + w * 40 + 2 * e, 20)

        @pl.when(b == 3)
        def _():
            columns()

        @pl.when((w == 1) & (k < 3))
        def _():
            zs[pl.ds(k, 1), 0:80] = pv[32:112, :].astype(BF)[None]
            rows_to(g, zs.at[k, 0:80], rz.at[me, 0:80], r_rz)

        @pl.when(b == 6)
        def _():
            zs[3, 0:48] = pv[32:80, :].astype(BF)
            rows_to(3, zs.at[3, 0:48], rz.at[me, 0:48], r_rz)

        @pl.when(b == 7)
        def _():
            zs[3, 48:96] = pv[72:120, :].astype(BF)
            rows_to(3, zs.at[3, 48:96], rz.at[me, 48:96], r_rw)

        @pl.when((w == 1) & (k == swap(s) + 2))
        def _():
            drain(rz.at[:, 0:80], r_rz)
            send_rows(0, True)
            send_rows(1, True)

        return carry

    lax.fori_loop(0, 8, pick, 0)

    swap_columns()

    @pl.when(s == 1)
    def _():
        drain(rz.at[:, 0:80], r_rz)
        send_rows(0, True)
        send_rows(1, True)

    @pl.when(s == 3)
    def _():
        drain(rz.at[:, 0:48], r_rz)
        send_rows(0, False)
        drain(rz.at[:, 48:96], r_rw)
        send_rows(1, False)

    drain_bytes(3 * 8192, s_val.at[1])
    for h in range(2):

        @pl.when(jnp.logical_not(twin & (core == h)))
        def _():
            drain(cond_ref.at[half(h)], s_cond.at[h])

    @pl.when(jnp.logical_not(twin))
    def _():
        drain(val_ref, s_val.at[0])
        drain(facs, s_fac)

    drain_bytes(2 * 65536, s_pass)

    drain_bytes(4 * 65536, s_sib)
    drain_bytes(6 * 16384 + 6 * 65536, s_vf)
    drain_bytes(7 * 4096, s_cb.at[1])

    @pl.when(core != zl)
    def _():
        drain_bytes(4096, s_cb.at[0])

    drain_bytes(15 * 16384, s_cx)
    drain(cx.at[:, core], s_cs)

    @pl.when(s < 3)
    def _():
        drain_bytes(316 * 1024, s_rz)

    @pl.when(s == 3)
    def _():
        drain_bytes(312 * 1024, s_rz)

    drain(cx.at[:, 1 - core], r_cs)
    drain_bytes(15 * 24576, r_rx)
    drain_bytes(15 * 24576, s_rx)


def on_device(val_orbitals, cond_orbitals, val_energy, cond_energy, plane_index, column_index):
    vmem = pl.BlockSpec(memory_space=pltpu.VMEM)
    smem = pl.BlockSpec(memory_space=pltpu.SMEM)
    dma = lambda *n: pltpu.SemaphoreType.DMA(n) if n else pltpu.SemaphoreType.DMA
    rx, cx = pl.pallas_call(
        kernel,
        out_shape=(
            jax.ShapeDtypeStruct((16, 32, 384), BF),
            jax.ShapeDtypeStruct((16, 2, 16, 512), BF),
        ),
        in_specs=[vmem, vmem, smem, smem] + [vmem] * 6,
        out_specs=(vmem, vmem),
        scratch_shapes=[
            pltpu.VMEM((32, 128), BF),
            pltpu.VMEM((32, 128), F32),
            pltpu.VMEM((4, 2, 4, 2, 32, 128), BF),
            pltpu.VMEM((4, 512, 128), BF),
            pltpu.VMEM((8, 128), F32),
            pltpu.VMEM((8, 128), F32),
            pltpu.VMEM((176, 128), jnp.int32),
            pltpu.VMEM((6, 176, 128), F32),
            pltpu.VMEM((4096, 128), F32),
            pltpu.VMEM((512, 512), BF),
            pltpu.VMEM((8, 256), F32),
            pltpu.VMEM((128, 128), F32),
            pltpu.VMEM((64, 128), F32),
            pltpu.VMEM((4, 96, 128), BF),
            pltpu.VMEM((16, 96, 128), BF),
            pltpu.VMEM((1280, 128), F32),
            pltpu.VMEM((16, 32, 384), BF),
            dma(2), dma(), dma(2), dma(4), dma(), dma(), dma(4), dma(), dma(),
            dma(), dma(), dma(), dma(4), dma(),
            dma(2), dma(), dma(), dma(), dma(), dma(), dma(), dma(), dma(), dma(), dma(),
        ],
        compiler_params=pltpu.CompilerParams(
            collective_id=0, has_side_effects=True, vmem_limit_bytes=48 * 2**20
        ),
        name="polarizability",
    )(
        val_orbitals,
        cond_orbitals.reshape(512, 128),
        val_energy,
        cond_energy,
        plane_index.reshape(156, 128),
        column_index.reshape(16, 128),
        *[jnp.asarray(t) for t in tables()],
    )
    return lax.dot_general(
        rx.reshape(512, 384)[:, :ROWS], cx.reshape(512, 512), (((0,), (0,)), ((), ())),
        preferred_element_type=F32,
    )


def solution(mesh):
    placed = (P("val", "cond"), P("cond", "val"), P("val"), P("cond"), P(), P())
    return jax.shard_map(
        on_device, mesh=mesh, in_specs=placed, out_specs=P("cond", "val"), check_vma=False
    )
```

time: 507 us -> 55.9 us (0.11)
  local copies, waits for them, and re-layouts: 225 us -> 0.04 us
  blocking collectives: 180 us -> 0 us
  Pallas kernels: 0 us -> 51.4 us
  waiting for transfers between devices: 35.2 us -> 0 us
  matrix products: 20.5 us -> 1.18 us
  between operations: 15 us -> 1.42 us
  starting transfers between devices: 12.3 us -> 0 us
  other arithmetic: 13.9 us -> 1.76 us
    gather x3 -> x0, local copies, waits for them, and re-layouts: 214 us -> none  [the longest x1 103 us: on_device(): picked_real = jnp.take(real_part, plane_index, axis=1)]
    all_gather x3 -> x0, blocking collectives: 180 us -> none  [the longest x1 79.7 us: on_device(): whole_val = lax.all_gather(val_orbitals, 'cond', axis=1, tiled=True)]
    pallas_call x0 -> x1, Pallas kernels: none -> 51.4 us  [on_device(): pl.pallas_call(kernel, out_shape=(jax.ShapeDtypeStruct((16, 32, 384), BF)...]
    reduce_scatter x1 -> x0, waiting for transfers between devices: 35.2 us -> none  [on_device(): lax.psum_scatter(partial_block.astype(jnp.bfloat16), 'val', scatter_dimen...]
    dot_general x11 -> x1, matrix products: 20.5 us -> 1.18 us  [on_device(): lax.dot_general(rx.reshape(512, 384)[:, :ROWS], cx.reshape(512, 512), (((...]
    all_to_all x1 -> x0, starting transfers between devices: 12.3 us -> none  [on_device(): lax.all_to_all(values, 'cond', split_axis=1, concat_axis=0, tiled=True)]
    mul x1 -> x0, other arithmetic: 10.9 us -> none  [on_device(): whole_val.astype(jnp.float32)[:, None, :]]
  transfers between devices with their start and end apart: 2 -> 0, of which waited for: 1 -> 0; matrix products, arithmetic and copies ran while one was open for 3% -> 0% of each run, Pallas kernels for 0% -> 0%
where the time goes in v1:
time: 55.9 us; the launch traced here: 55.8 us
  Pallas kernels  51.4 us (92%)
  other arithmetic  1.76 us (3%)
  between operations  1.42 us (3%)
  matrix products  1.18 us (2%)
    pallas_call x1, Pallas kernels, on_device(): pl.pallas_call(kernel, out_shape=(jax.ShapeDtypeStruct((16, 32, 384), BF)...  51.4 us
    unnamed x1, other arithmetic  1.76 us
    dot_general x1, matrix products, on_device(): lax.dot_general(rx.reshape(512, 384)[:, :ROWS], cx.reshape(512, 512), (((...  1.18 us

profile of v1, /device:TPU:33, one launch (start us, length us, event | category | flops | bytes accessed | tf_op | source)
XLA Modules:
  0.0 55.8 jit_solution(14514214139761532140)
XLA Ops:
  1.3 0.0 copy-start
  1.3 0.0 copy-start.1
  1.3 0.0 copy-start.2
  1.3 0.0 copy-start.3
  1.3 0.0 copy-start.4
  1.4 0.0 copy-start.5
  1.4 0.0 copy-start.6
  1.4 1.8 %reduce = bf16[65536]{0:T(1024)(128)(2,1)S(1)} reduce(bf16[1,65536]{1,0:T(2,128)(2,1)} %param.11, bf16[]{:T(256)} %constant.16), dimensions={0}, to_apply=%param.11.reduce_sub_computation | reduce | bytes 262146 | tf_op args[1]
  3.1 0.0 copy-done
  3.2 0.0 copy-done.1
  3.2 0.0 copy-done.2
  3.2 0.0 copy-done.3
  3.2 0.0 copy-done.4
  3.2 0.0 copy-done.5
  3.2 0.0 copy-done.6
  3.2 51.4 %polarizability.1 = (bf16[16,32,384]{2,1,0:T(8,128)(2,1)S(1)}, bf16[16,2,16,512]{3,2,1,0:T(8,128)(2,1)S(1)}) custom-call(bf16[1,4096]{1,0:T(2,128)(2,1)S(1)} %copy-done.5, bf16[512,128]{1,0:T(8,128)(2,1)S(1)} %bitcast.7, f32[1]{0:T(128)S(6)} %copy.11.ve_ref, f32[1]{0:T(128)S(6)} %copy.12.ce_ref, s32[156,128]{1,0:T(8,128)S(1)} %bitcast.9, ...), custom_call_target="tpu_custom_call" | custom-call | tf_op jit(solution)/shard_map/polarizability/pallas_call | solution.py:534
  54.6 1.2 %fusion = f32[312,512]{1,0:T(8,128)} fusion(bf16[512,512]{1,0:T(8,128)(2,1)S(1)} %bitcast.6, bf16[512,384]{1,0:T(8,128)(2,1)S(1)} %bitcast.8), kind=kOutput, calls=%fused_computation | convolution fusion | flops 163577856 | bytes 1556480 | tf_op jit(solution)/shard_map/dot_general | solution.py:577
Async XLA Ops:
  1.3 1.8 %copy-start = (bf16[256,256]{1,0:T(8,128)(2,1)S(1)}, bf16[256,256]{1,0:T(8,128)(2,1)}, u32[]{:S(2)}) copy-start(bf16[256,256]{1,0:T(8,128)(2,1)} %constant.8.clone.tz) | copy-start | bytes 393220
  1.3 1.8 %copy-start.1 = (s32[19968]{0:T(1024)S(1)}, s32[19968]{0:T(1024)}, u32[]{:S(2)}) copy-start(s32[19968]{0:T(1024)} %param.14) | copy-start | bytes 239620
  1.3 1.8 %copy-start.2 = (bf16[80,256]{1,0:T(8,128)(2,1)S(1)}, bf16[80,256]{1,0:T(8,128)(2,1)}, u32[]{:S(2)}) copy-start(bf16[80,256]{1,0:T(8,128)(2,1)} %constant.10.clone.tx) | copy-start | bytes 122884
  1.3 1.8 %copy-start.3 = (f32[2,32,128]{2,1,0:T(8,128)S(1)}, f32[2,32,128]{2,1,0:T(8,128)}, u32[]{:S(2)}) copy-start(f32[2,32,128]{2,1,0:T(8,128)} %constant.11.clone.tw) | copy-start | bytes 98308
  1.3 1.8 %copy-start.4 = (bf16[64,192]{1,0:T(8,128)(2,1)S(1)}, bf16[64,192]{1,0:T(8,128)(2,1)}, u32[]{:S(2)}) copy-start(bf16[64,192]{1,0:T(8,128)(2,1)} %constant.9.clone.ty) | copy-start | bytes 73732
  1.4 1.8 %copy-start.5 = (bf16[1,4096]{1,0:T(2,128)(2,1)S(1)}, bf16[1,4096]{1,0:T(2,128)(2,1)}, u32[]{:S(2)}) copy-start(bf16[1,4096]{1,0:T(2,128)(2,1)} %val_in.1) | copy-start | bytes 24580
  1.4 1.8 %copy-start.6 = (s32[2048]{0:T(1024)S(1)}, s32[2048]{0:T(1024)}, u32[]{:S(2)}) copy-start(s32[2048]{0:T(1024)} %param.15) | copy-start | bytes 24580

commit v2 on v1

--- a/solution.py
+++ b/solution.py
@@ -107,7 +107,7 @@
         ix_ref[pl.ds(2 * t + 1, 1), :] = flat[:, 128:]
         return carry
 
-    lax.fori_loop(0, 8, tile, 0, unroll=4)
+    lax.fori_loop(0, 8, tile, 0, unroll=8)
 
 
 def fold_indices(ix_ref, fx_ref):
@@ -214,7 +214,7 @@
             wt[rows, pl.ds(pl.multiple_of((i % 4) * 128, 128), 128)] = whole
         return carry
 
-    lax.fori_loop(0, 8, lines, 0, unroll=2)
+    lax.fori_loop(0, 8, lines, 0, unroll=4)
 
 
 def pick_tile(t, fx, wt, sp):

time: 55.9 us -> 55.5 us (level)
  no operation moved by 1% of the time
where the time goes in v2:
time: 55.5 us; the launch traced here: 55.4 us
  Pallas kernels  51 us (92%)
  other arithmetic  1.76 us (3%)
  between operations  1.42 us (3%)
  matrix products  1.18 us (2%)
    pallas_call x1, Pallas kernels, on_device(): pl.pallas_call(kernel, out_shape=(jax.ShapeDtypeStruct((16, 32, 384), BF)...  51 us
    unnamed x1, other arithmetic  1.76 us
    dot_general x1, matrix products, on_device(): lax.dot_general(rx.reshape(512, 384)[:, :ROWS], cx.reshape(512, 512), (((...  1.18 us

profile of v2, /device:TPU:33, one launch (start us, length us, event | category | flops | bytes accessed | tf_op | source)
XLA Modules:
  0.0 55.4 jit_solution(4221012217036024275)
XLA Ops:
  1.3 0.0 copy-start
  1.3 0.0 copy-start.1
  1.3 0.0 copy-start.2
  1.3 0.0 copy-start.3
  1.3 0.0 copy-start.4
  1.4 0.0 copy-start.5
  1.4 0.0 copy-start.6
  1.4 1.8 %reduce = bf16[65536]{0:T(1024)(128)(2,1)S(1)} reduce(bf16[1,65536]{1,0:T(2,128)(2,1)} %param.11, bf16[]{:T(256)} %constant.16), dimensions={0}, to_apply=%param.11.reduce_sub_computation | reduce | bytes 262146 | tf_op args[1]
  3.1 0.0 copy-done
  3.2 0.0 copy-done.1
  3.2 0.0 copy-done.2
  3.2 0.0 copy-done.3
  3.2 0.0 copy-done.4
  3.2 0.0 copy-done.5
  3.2 0.0 copy-done.6
  3.2 51.0 %polarizability.1 = (bf16[16,32,384]{2,1,0:T(8,128)(2,1)S(1)}, bf16[16,2,16,512]{3,2,1,0:T(8,128)(2,1)S(1)}) custom-call(bf16[1,4096]{1,0:T(2,128)(2,1)S(1)} %copy-done.5, bf16[512,128]{1,0:T(8,128)(2,1)S(1)} %bitcast.7, f32[1]{0:T(128)S(6)} %copy.11.ve_ref, f32[1]{0:T(128)S(6)} %copy.12.ce_ref, s32[156,128]{1,0:T(8,128)S(1)} %bitcast.9, ...), custom_call_target="tpu_custom_call" | custom-call | tf_op jit(solution)/shard_map/polarizability/pallas_call | solution.py:534
  54.2 1.2 %fusion = f32[312,512]{1,0:T(8,128)} fusion(bf16[512,512]{1,0:T(8,128)(2,1)S(1)} %bitcast.6, bf16[512,384]{1,0:T(8,128)(2,1)S(1)} %bitcast.8), kind=kOutput, calls=%fused_computation | convolution fusion | flops 163577856 | bytes 1556480 | tf_op jit(solution)/shard_map/dot_general | solution.py:577
Async XLA Ops:
  1.3 1.8 %copy-start = (bf16[256,256]{1,0:T(8,128)(2,1)S(1)}, bf16[256,256]{1,0:T(8,128)(2,1)}, u32[]{:S(2)}) copy-start(bf16[256,256]{1,0:T(8,128)(2,1)} %constant.8.clone.tz) | copy-start | bytes 393220
  1.3 1.8 %copy-start.1 = (s32[19968]{0:T(1024)S(1)}, s32[19968]{0:T(1024)}, u32[]{:S(2)}) copy-start(s32[19968]{0:T(1024)} %param.14) | copy-start | bytes 239620
  1.3 1.8 %copy-start.2 = (bf16[80,256]{1,0:T(8,128)(2,1)S(1)}, bf16[80,256]{1,0:T(8,128)(2,1)}, u32[]{:S(2)}) copy-start(bf16[80,256]{1,0:T(8,128)(2,1)} %constant.10.clone.tx) | copy-start | bytes 122884
  1.3 1.8 %copy-start.3 = (f32[2,32,128]{2,1,0:T(8,128)S(1)}, f32[2,32,128]{2,1,0:T(8,128)}, u32[]{:S(2)}) copy-start(f32[2,32,128]{2,1,0:T(8,128)} %constant.11.clone.tw) | copy-start | bytes 98308
  1.3 1.8 %copy-start.4 = (bf16[64,192]{1,0:T(8,128)(2,1)S(1)}, bf16[64,192]{1,0:T(8,128)(2,1)}, u32[]{:S(2)}) copy-start(bf16[64,192]{1,0:T(8,128)(2,1)} %constant.9.clone.ty) | copy-start | bytes 73732
  1.4 1.8 %copy-start.5 = (bf16[1,4096]{1,0:T(2,128)(2,1)S(1)}, bf16[1,4096]{1,0:T(2,128)(2,1)}, u32[]{:S(2)}) copy-start(bf16[1,4096]{1,0:T(2,128)(2,1)} %val_in.1) | copy-start | bytes 24580
  1.4 1.8 %copy-start.6 = (s32[2048]{0:T(1024)S(1)}, s32[2048]{0:T(1024)}, u32[]{:S(2)}) copy-start(s32[2048]{0:T(1024)} %param.15) | copy-start | bytes 24580

commit v3 on v2

--- a/solution.py
+++ b/solution.py
@@ -474,7 +474,9 @@
 
     lax.fori_loop(0, 8, pick, 0)
 
-    swap_columns()
+    @pl.when((s & 1) == 0)
+    def _():
+        swap_columns()
 
     @pl.when(s == 1)
     def _():
@@ -488,6 +490,10 @@
         send_rows(0, False)
         drain(rz.at[:, 48:96], r_rw)
         send_rows(1, False)
+
+    @pl.when((s & 1) == 1)
+    def _():
+        swap_columns()
 
     drain_bytes(3 * 8192, s_val.at[1])
     for h in range(2):

time: 55.5 us -> 55.5 us (level)
  no operation moved by 1% of the time
where the time goes in v3:
time: 55.5 us; the launch traced here: 55.4 us
  Pallas kernels  51 us (92%)
  other arithmetic  1.76 us (3%)
  between operations  1.42 us (3%)
  matrix products  1.18 us (2%)
    pallas_call x1, Pallas kernels, on_device(): pl.pallas_call(kernel, out_shape=(jax.ShapeDtypeStruct((16, 32, 384), BF)...  51 us
    unnamed x1, other arithmetic  1.76 us
    dot_general x1, matrix products, on_device(): lax.dot_general(rx.reshape(512, 384)[:, :ROWS], cx.reshape(512, 512), (((...  1.18 us

profile of v3, /device:TPU:33, one launch (start us, length us, event | category | flops | bytes accessed | tf_op | source)
XLA Modules:
  0.0 55.4 jit_solution(2126613728773081910)
XLA Ops:
  1.3 0.0 copy-start
  1.3 0.0 copy-start.1
  1.3 0.0 copy-start.2
  1.3 0.0 copy-start.3
  1.3 0.0 copy-start.4
  1.4 0.0 copy-start.5
  1.4 0.0 copy-start.6
  1.4 1.8 %reduce = bf16[65536]{0:T(1024)(128)(2,1)S(1)} reduce(bf16[1,65536]{1,0:T(2,128)(2,1)} %param.11, bf16[]{:T(256)} %constant.16), dimensions={0}, to_apply=%param.11.reduce_sub_computation | reduce | bytes 262146 | tf_op args[1]
  3.1 0.0 copy-done
  3.2 0.0 copy-done.1
  3.2 0.0 copy-done.2
  3.2 0.0 copy-done.3
  3.2 0.0 copy-done.4
  3.2 0.0 copy-done.5
  3.2 0.0 copy-done.6
  3.2 51.0 %polarizability.1 = (bf16[16,32,384]{2,1,0:T(8,128)(2,1)S(1)}, bf16[16,2,16,512]{3,2,1,0:T(8,128)(2,1)S(1)}) custom-call(bf16[1,4096]{1,0:T(2,128)(2,1)S(1)} %copy-done.5, bf16[512,128]{1,0:T(8,128)(2,1)S(1)} %bitcast.7, f32[1]{0:T(128)S(6)} %copy.11.ve_ref, f32[1]{0:T(128)S(6)} %copy.12.ce_ref, s32[156,128]{1,0:T(8,128)S(1)} %bitcast.9, ...), custom_call_target="tpu_custom_call" | custom-call | tf_op jit(solution)/shard_map/polarizability/pallas_call | solution.py:540
  54.2 1.2 %fusion = f32[312,512]{1,0:T(8,128)} fusion(bf16[512,512]{1,0:T(8,128)(2,1)S(1)} %bitcast.6, bf16[512,384]{1,0:T(8,128)(2,1)S(1)} %bitcast.8), kind=kOutput, calls=%fused_computation | convolution fusion | flops 163577856 | bytes 1556480 | tf_op jit(solution)/shard_map/dot_general | solution.py:583
Async XLA Ops:
  1.3 1.8 %copy-start = (bf16[256,256]{1,0:T(8,128)(2,1)S(1)}, bf16[256,256]{1,0:T(8,128)(2,1)}, u32[]{:S(2)}) copy-start(bf16[256,256]{1,0:T(8,128)(2,1)} %constant.8.clone.tz) | copy-start | bytes 393220
  1.3 1.8 %copy-start.1 = (s32[19968]{0:T(1024)S(1)}, s32[19968]{0:T(1024)}, u32[]{:S(2)}) copy-start(s32[19968]{0:T(1024)} %param.14) | copy-start | bytes 239620
  1.3 1.8 %copy-start.2 = (bf16[80,256]{1,0:T(8,128)(2,1)S(1)}, bf16[80,256]{1,0:T(8,128)(2,1)}, u32[]{:S(2)}) copy-start(bf16[80,256]{1,0:T(8,128)(2,1)} %constant.10.clone.tx) | copy-start | bytes 122884
  1.3 1.8 %copy-start.3 = (f32[2,32,128]{2,1,0:T(8,128)S(1)}, f32[2,32,128]{2,1,0:T(8,128)}, u32[]{:S(2)}) copy-start(f32[2,32,128]{2,1,0:T(8,128)} %constant.11.clone.tw) | copy-start | bytes 98308
  1.3 1.8 %copy-start.4 = (bf16[64,192]{1,0:T(8,128)(2,1)S(1)}, bf16[64,192]{1,0:T(8,128)(2,1)}, u32[]{:S(2)}) copy-start(bf16[64,192]{1,0:T(8,128)(2,1)} %constant.9.clone.ty) | copy-start | bytes 73732
  1.4 1.8 %copy-start.5 = (bf16[1,4096]{1,0:T(2,128)(2,1)S(1)}, bf16[1,4096]{1,0:T(2,128)(2,1)}, u32[]{:S(2)}) copy-start(bf16[1,4096]{1,0:T(2,128)(2,1)} %val_in.1) | copy-start | bytes 24580
  1.4 1.8 %copy-start.6 = (s32[2048]{0:T(1024)S(1)}, s32[2048]{0:T(1024)}, u32[]{:S(2)}) copy-start(s32[2048]{0:T(1024)} %param.15) | copy-start | bytes 24580

commit v4 on v2

--- a/solution.py
+++ b/solution.py
@@ -214,7 +214,7 @@
             wt[rows, pl.ds(pl.multiple_of((i % 4) * 128, 128), 128)] = whole
         return carry
 
-    lax.fori_loop(0, 8, lines, 0, unroll=4)
+    lax.fori_loop(0, 8, lines, 0, unroll=8)
 
 
 def pick_tile(t, fx, wt, sp):
@@ -318,6 +318,7 @@
             s_cond.at[h], r_cond.at[p], s, at_s(near * 2 + h),
         )
 
+    order_planes(plane_ref, ix)
     drain(vf.at[y, :, x], r_val)
     for k in range(1, 4):
         remote(vf.at[y, 0, x], vf.at[y, 0, x], s_vf, r_va, p, by_xy(k)).start()
@@ -341,7 +342,6 @@
 
     pass_on(0)
     pass_on(1)
-    order_planes(plane_ref, ix)
     compose_columns(plane_ref, col_ref, ix)
     fold_indices(ix, fx)
     pass_on(2)

time: 55.5 us -> 54.2 us (0.977)
  Pallas kernels: 51 us -> 49.6 us
    pallas_call x1, Pallas kernels: 51 us -> 49.6 us  [on_device(): pl.pallas_call(kernel, out_shape=(jax.ShapeDtypeStruct((16, 32, 384), BF)...]
where the time goes in v4:
time: 54.2 us; the launch traced here: 54 us
  Pallas kernels  49.6 us (92%)
  other arithmetic  1.76 us (3%)
  between operations  1.42 us (3%)
  matrix products  1.18 us (2%)
    pallas_call x1, Pallas kernels, on_device(): pl.pallas_call(kernel, out_shape=(jax.ShapeDtypeStruct((16, 32, 384), BF)...  49.6 us
    unnamed x1, other arithmetic  1.76 us
    dot_general x1, matrix products, on_device(): lax.dot_general(rx.reshape(512, 384)[:, :ROWS], cx.reshape(512, 512), (((...  1.18 us

profile of v4, /device:TPU:33, one launch (start us, length us, event | category | flops | bytes accessed | tf_op | source)
XLA Modules:
  0.0 54.0 jit_solution(17976246586259439451)
XLA Ops:
  1.3 0.0 copy-start
  1.3 0.0 copy-start.1
  1.3 0.0 copy-start.2
  1.3 0.0 copy-start.3
  1.3 0.0 copy-start.4
  1.4 0.0 copy-start.5
  1.4 0.0 copy-start.6
  1.4 1.8 %reduce = bf16[65536]{0:T(1024)(128)(2,1)S(1)} reduce(bf16[1,65536]{1,0:T(2,128)(2,1)} %param.11, bf16[]{:T(256)} %constant.16), dimensions={0}, to_apply=%param.11.reduce_sub_computation | reduce | bytes 262146 | tf_op args[1]
  3.1 0.0 copy-done
  3.2 0.0 copy-done.1
  3.2 0.0 copy-done.2
  3.2 0.0 copy-done.3
  3.2 0.0 copy-done.4
  3.2 0.0 copy-done.5
  3.2 0.0 copy-done.6
  3.2 49.6 %polarizability.1 = (bf16[16,32,384]{2,1,0:T(8,128)(2,1)S(1)}, bf16[16,2,16,512]{3,2,1,0:T(8,128)(2,1)S(1)}) custom-call(bf16[1,4096]{1,0:T(2,128)(2,1)S(1)} %copy-done.5, bf16[512,128]{1,0:T(8,128)(2,1)S(1)} %bitcast.7, f32[1]{0:T(128)S(6)} %copy.11.ve_ref, f32[1]{0:T(128)S(6)} %copy.12.ce_ref, s32[156,128]{1,0:T(8,128)S(1)} %bitcast.9, ...), custom_call_target="tpu_custom_call" | custom-call | tf_op jit(solution)/shard_map/polarizability/pallas_call | solution.py:534
  52.9 1.2 %fusion = f32[312,512]{1,0:T(8,128)} fusion(bf16[512,512]{1,0:T(8,128)(2,1)S(1)} %bitcast.6, bf16[512,384]{1,0:T(8,128)(2,1)S(1)} %bitcast.8), kind=kOutput, calls=%fused_computation | convolution fusion | flops 163577856 | bytes 1556480 | tf_op jit(solution)/shard_map/dot_general | solution.py:577
Async XLA Ops:
  1.3 1.8 %copy-start = (bf16[256,256]{1,0:T(8,128)(2,1)S(1)}, bf16[256,256]{1,0:T(8,128)(2,1)}, u32[]{:S(2)}) copy-start(bf16[256,256]{1,0:T(8,128)(2,1)} %constant.8.clone.tz) | copy-start | bytes 393220
  1.3 1.8 %copy-start.1 = (s32[19968]{0:T(1024)S(1)}, s32[19968]{0:T(1024)}, u32[]{:S(2)}) copy-start(s32[19968]{0:T(1024)} %param.14) | copy-start | bytes 239620
  1.3 1.8 %copy-start.2 = (bf16[80,256]{1,0:T(8,128)(2,1)S(1)}, bf16[80,256]{1,0:T(8,128)(2,1)}, u32[]{:S(2)}) copy-start(bf16[80,256]{1,0:T(8,128)(2,1)} %constant.10.clone.tx) | copy-start | bytes 122884
  1.3 1.8 %copy-start.3 = (f32[2,32,128]{2,1,0:T(8,128)S(1)}, f32[2,32,128]{2,1,0:T(8,128)}, u32[]{:S(2)}) copy-start(f32[2,32,128]{2,1,0:T(8,128)} %constant.11.clone.tw) | copy-start | bytes 98308
  1.3 1.8 %copy-start.4 = (bf16[64,192]{1,0:T(8,128)(2,1)S(1)}, bf16[64,192]{1,0:T(8,128)(2,1)}, u32[]{:S(2)}) copy-start(bf16[64,192]{1,0:T(8,128)(2,1)} %constant.9.clone.ty) | copy-start | bytes 73732
  1.4 1.8 %copy-start.5 = (bf16[1,4096]{1,0:T(2,128)(2,1)S(1)}, bf16[1,4096]{1,0:T(2,128)(2,1)}, u32[]{:S(2)}) copy-start(bf16[1,4096]{1,0:T(2,128)(2,1)} %val_in.1) | copy-start | bytes 24580
  1.4 1.8 %copy-start.6 = (s32[2048]{0:T(1024)S(1)}, s32[2048]{0:T(1024)}, u32[]{:S(2)}) copy-start(s32[2048]{0:T(1024)} %param.15) | copy-start | bytes 24580
